TPU v7x, 32 devices: a whole 2x2x4 slice. The times are simulated.
32 devices in a mesh: ang: 4 (over y, x), pix: 8 (over z, core).
Axes of the slice: x: 2, y: 2, z: 4, core: 2. Of those that a mesh axis runs over, the one named last changes fastest.
Arguments:
- flats: float32 [256, 64, 4096], P(None, 'pix', 'ang'), may hold values from -60 to 60
- projections: float32 [128, 64, 4096], P('ang', None, 'pix'), may hold values from -60 to 60
- start_basis: float32 [256, 48], replicated, may hold values from -0.375 to 0.375
Outputs:
- corrected: float32 [128, 64, 4096], P('ang', None, 'pix')
All inputs are finite; a program needn't handle non-finite values.
Results may differ from a plain program's by a relative error of at most 0.0001.
Values sent between devices are 32-bit elements; how exact they have to be, the bound alone decides.
A program may use at most 128 MiB of HBM per device.

v0:
```python
import jax
import jax.numpy as jnp
from jax import lax
from jax.sharding import PartitionSpec as P

SUBSPACE = 2


floor_value = 0.2


def orthonormal(grown):
    correlation = jnp.dot(grown.T, grown, precision=lax.Precision.HIGHEST)
    lower = jnp.linalg.cholesky(correlation)
    return jax.scipy.linalg.solve_triangular(lower, grown.T, lower=True).T


def solve_normal(normal, fit_rhs):
    factor = jnp.linalg.cholesky(normal)
    return jax.scipy.linalg.cho_solve((factor, True), fit_rhs.T).T


def shards(flats, projections, start_basis):
    frames_here, rows_dev, cols_dev = flats.shape
    npix = rows_dev * cols_dev * lax.axis_size("ang") * lax.axis_size("pix")
    mean_flat = jnp.mean(flats, axis=0)
    centered = (flats - mean_flat).reshape(frames_here, -1)
    local_gram = jnp.dot(centered, centered.T, precision=lax.Precision.HIGHEST)
    gram = lax.psum(local_gram, ("ang", "pix")) / npix
    basis = start_basis
    for turn in range(SUBSPACE):
        basis = orthonormal(jnp.dot(gram, basis, precision=lax.Precision.HIGHEST))
    eigen_flats = jnp.dot(basis.T, centered, precision=lax.Precision.HIGHEST)
    normal = jnp.dot(
        basis.T,
        jnp.dot(gram, basis, precision=lax.Precision.HIGHEST),
        precision=lax.Precision.HIGHEST,
    )
    eigen_count = eigen_flats.shape[0]
    tiles = lax.all_to_all(projections, "pix", split_axis=1, concat_axis=2, tiled=True)
    eigen_rows, mean_rows = (
        lax.all_gather(
            eigen_flats.reshape(eigen_count, rows_dev, cols_dev), "ang", axis=2, tiled=True
        ),
        lax.all_gather(mean_flat, "ang", axis=1, tiled=True),
    )
    angle_count = tiles.shape[0]
    frames = tiles.reshape(angle_count, -1)
    flat_row = mean_rows.reshape(1, -1)
    eigen_wide = eigen_rows.reshape(eigen_count, -1)
    partial_value = jnp.dot(frames - flat_row, eigen_wide.T, precision=lax.Precision.HIGHEST)
    fit_rhs = lax.psum(partial_value, "pix") / npix
    weights = solve_normal(normal, fit_rhs)
    estimate = flat_row + jnp.dot(weights, eigen_wide, precision=lax.Precision.HIGHEST)
    tiles_out = (frames / jnp.maximum(estimate, floor_value)).reshape(tiles.shape)
    result = lax.all_to_all(tiles_out, "pix", split_axis=2, concat_axis=1, tiled=True)
    return result


def solution(mesh):
    in_specs = (P(None, "pix", "ang"), P("ang", None, "pix"), P())
    out_specs = P("ang", None, "pix")
    return jax.shard_map(shards, mesh=mesh, in_specs=in_specs, out_specs=out_specs, check_vma=False)
```

profile of v0, /device:TPU:0, one launch (start us, length us, event | category | flops | bytes accessed | tf_op | source)
XLA Modules:
  0.0 540.1 jit_solution(17310506107402112178)
XLA Ops:
  6.5 3.9 reduce_sum.9
  10.5 4.4 broadcast_subtract_fusion
  14.8 3.2 copy-done.2
  18.1 17.3 %fusion.4 = f32[256,256]{1,0:T(8,128)} fusion(f32[256,8,1024]{2,1,0:T(8,128)S(1)} %broadcast_subtract_fusion), kind=kOutput, calls=%fused_computation.7 | convolution fusion | flops 6442450944 | bytes 8650752 | tf_op jit(solution)/shard_map/dot_general | solution.py:28
  35.4 0.6 all-gather.2.cloned.1.call-start
  36.0 15.0 %copy.49 = f32[32,8,8,1024]{3,1,2,0:T(8,128)} copy(f32[32,8,8,1024]{3,2,1,0:T(8,128)} %bitcast.82) | data formatting | bytes 16777216
  51.0 9.2 %copy.41 = f32[8192,256]{1,0:T(8,128)} copy(f32[8192,256]{0,1:T(8,128)} %bitcast.86) | data formatting | bytes 16777216 | tf_op jit(solution)/shard_map/dot_general | solution.py:33
  60.1 103.0 %all-reduce.2.cloned.1.call-done = f32[256,256]{1,0:T(8,128)} async-done(((f32[256,256]{1,0:T(8,128)}), f32[256,256]{1,0:T(8,128)}) %all-reduce.2.cloned.1.call-update) | async-done | bytes 262160 | tf_op jit(solution)/shard_map/psum | solution.py:29
  163.2 1.3 fusion.11
  164.7 4.4 cholesky.59
  169.2 0.6 compare_reduce_fusion.2
  169.8 0.7 fusion.22
  170.5 3.7 custom-call.14
  174.1 0.2 fusion.20
  174.4 1.3 fusion.9
  176.0 4.4 cholesky.70
  180.4 0.6 compare_reduce_fusion.1
  181.0 0.7 fusion.23
  181.7 3.7 custom-call.15
  185.4 0.2 fusion.18
  185.6 12.2 %fusion.16 = f32[48,8,1024]{2,0,1:T(8,128)} fusion(f32[8,1024,256]{2,1,0:T(8,128)} %bitcast.85, f32[48,256]{1,0:T(8,128)S(1)} %fusion.18), kind=kOutput, calls=%fused_computation.17 | convolution fusion | flops 1207959552 | bytes 10010624 | tf_op jit(solution)/shard_map/dot_general | solution.py:33
  197.8 6.7 %copy.33 = f32[32,64,512]{2,0,1:T(8,128)} copy(f32[32,64,512]{2,1,0:T(8,128)} %param.7) | data formatting | bytes 8388608 | tf_op args[1]
  204.6 4.8 all-to-all-start
  209.4 9.4 %all_gather.6 = f32[8,4096]{1,0:T(8,128)S(1)} all-gather(f32[8,1024]{1,0:T(8,128)S(1)} %broadcast_multiply_fusion), channel_id=1, replica_groups=mesh['ang'=4,'pix'=8] {'ang'}, dimensions={1}, use_global_device_ids=true | all-gather | bytes 163840 | tf_op jit(solution)/shard_map/all_gather | solution.py:45
  219.0 0.4 fusion.7
  219.6 4.4 cholesky.81
  224.0 0.7 compare_reduce_fusion
  224.7 0.7 fusion.24
  225.4 3.7 custom-call.12
  229.1 74.3 %all-to-all-done = f32[32,64,512]{2,0,1:T(8,128)} async-done(((f32[32,64,512]{2,0,1:T(8,128)}), f32[32,64,512]{2,0,1:T(8,128)}, u32[]{:S(2)}, u32[]{:S(2)}) %all-to-all-start) | async-done | bytes 4194336 | tf_op jit(solution)/shard_map/all_to_all | solution.py:40
  303.4 4.6 copy.34
  308.0 4.6 bitcast_subtract_fusion
  312.7 4.5 copy.48
  317.1 4.4 copy.46
  321.6 0.4 copy-start.4
  322.0 3.3 copy.45
  325.3 2.7 copy-done.3
  328.0 5.1 fusion.47
  333.0 26.7 %psum.15 = f32[32,48]{1,0:T(8,128)S(1)} all-reduce(f32[32,48]{1,0:T(8,128)S(1)} %fusion.47), channel_id=1, replica_groups=mesh['ang'=4,'pix'=8] {'pix'}, use_global_device_ids=true, to_apply=%region_4.7 | all-reduce | flops 1536 | bytes 12288 | tf_op jit(solution)/shard_map/psum | solution.py:52
  360.0 6.7 %fusion.1 = f32[32,32768]{1,0:T(8,128)S(1)} fusion(f32[32,32768]{1,0:T(8,128)} %bitcast.94, f32[48,32]{0,1:T(8,128)S(1)} %fusion.25, f32[48,32768]{1,0:T(8,128)} %bitcast.88, f32[32768]{0:T(1024)S(1)} %bitcast.98), kind=kOutput, calls=%fused_computation.2 | convolution fusion | flops 607125504 | bytes 14817280 | tf_op jit(solution)/shard_map/dot_general | solution.py:54
  366.7 4.4 copy.50
  371.2 10.8 %copy.43 = f32[32,8,4096]{0,1,2:T(8,128)} copy(f32[32,8,4096]{2,1,0:T(8,128)} %bitcast.90) | data formatting | bytes 8388608 | tf_op jit(solution)/shard_map/reshape | solution.py:55
  382.0 12.8 %reshape.47 = f32[8,1,131072]{2,1,0:T(1,128)} reshape(f32[4096,8,32]{2,1,0:T(8,128)} %bitcast.83) | data formatting | bytes 8388608
  394.8 98.7 %all_to_all.33 = f32[8,1,131072]{2,1,0:T(1,128)} all-to-all(f32[8,1,131072]{2,1,0:T(1,128)} %reshape.47), channel_id=1, replica_groups=mesh['ang'=4,'pix'=8] {'pix'}, dimensions={0} | all-to-all | bytes 8388608 | tf_op jit(solution)/shard_map/all_to_all | solution.py:56
  493.5 0.5 broadcast.81
  494.0 13.7 %reduce.4 = f32[8,131072]{1,0:T(8,128)} reduce(f32[8,1,131072]{2,1,0:T(1,128)} %all_to_all.33, f32[]{:T(128)} %broadcast.81), dimensions={1}, to_apply=%all_to_all.27.reduce_sub_computation | reduce | bytes 8388612 | tf_op jit(solution)/shard_map/all_to_all | solution.py:56
  507.8 13.3 %reshape.48 = f32[4096,8,32]{2,1,0:T(8,128)} reshape(f32[8,131072]{1,0:T(8,128)} %reduce.4) | data formatting | bytes 8388608
  521.1 12.0 %copy.44 = f32[32,8,8,512]{3,2,1,0:T(8,128)} copy(f32[32,8,8,512]{0,2,3,1:T(8,128)} %bitcast.84) | data formatting | bytes 8388608 | tf_op jit(solution)/shard_map/all_to_all | solution.py:56
  (30 shorter events, 1.3 us)
Async XLA Ops:
  6.5 156.6 %copy-start = (f32[256,48]{0,1:T(8,128)S(1)}, f32[256,48]{0,1:T(8,128)}, u32[]{:S(2)}) copy-start(f32[256,48]{0,1:T(8,128)} %param.8) | copy-start | bytes 147460
  6.5 156.6 %all-reduce.2.cloned.1.call-start = ((), (), s32[]{:S(2)}) async-start(), calls=%async_computation.2 | async-start | bytes 524288 | tf_op jit(solution)/shard_map/psum | solution.py:29
  14.8 3.2 copy-start.2
  35.4 286.2 %all-gather.2.cloned.1.call-start = ((), (), s32[]{:S(2)}) async-start(), calls=%async_computation.3 | async-start | bytes 7864320 | tf_op jit(solution)/shard_map/all_gather | solution.py:42
  204.6 14.4 %copy-start.5 = (f32[256,256]{1,0:T(8,128)S(1)}, f32[256,256]{1,0:T(8,128)}, u32[]{:S(2)}) copy-start(f32[256,256]{1,0:T(8,128)} %all-reduce.2.cloned.1.call-done) | copy-start | bytes 786436
  204.6 98.8 %all-to-all-start = ((f32[32,64,512]{2,0,1:T(8,128)}), f32[32,64,512]{2,0,1:T(8,128)}, u32[]{:S(2)}, u32[]{:S(2)}) async-start(f32[32,64,512]{2,0,1:T(8,128)} %copy.33), calls=%async_computation | async-start | bytes 8388608 | tf_op jit(solution)/shard_map/all_to_all | solution.py:40
  321.6 6.4 %copy-start.4 = (f32[4,8,64,512]{3,1,2,0:T(8,128)S(1)}, f32[4,8,64,512]{3,1,2,0:T(8,128)}, u32[]{:S(2)}) copy-start(f32[4,8,64,512]{3,1,2,0:T(8,128)} %copy.48) | copy-start | bytes 12582916
  325.3 2.7 copy-start.3
  521.1 12.0 %copy-start.1 = (f32[256,48]{0,1:T(8,128)S(1)}, f32[256,48]{0,1:T(8,128)}, u32[]{:S(2)}) copy-start(f32[256,48]{0,1:T(8,128)} %param.8) | copy-start | bytes 147460
Sparse Core Ops, SparseCore 0:
  35.5 127.6 all-reduce.1
  198.0 70.4 all-gather.1
where the time goes:
time: 550 us; the launch traced here: 540 us
  waiting for transfers between devices  177 us (32%)
  blocking collectives  135 us (25%)
  local copies, waits for them, and re-layouts  108 us (20%)
  other arithmetic  54.9 us (10%)
  matrix products  45.5 us (8%)
  between operations  13.8 us (3%)
    psum x1, waiting for transfers between devices, shards(): gram = lax.psum(local_gram, ('ang', 'pix')) / npix  103 us
    all_to_all x1, blocking collectives, shards(): lax.all_to_all(tiles_out, 'pix', split_axis=2, concat_axis=1, tiled=True)  98.7 us
    all_to_all x1, waiting for transfers between devices, shards(): lax.all_to_all(projections, 'pix', split_axis=1, concat_axis=2, tiled=True)  74.3 us
    unnamed x20, local copies, waits for them, and re-layouts  67.5 us
    psum x1, blocking collectives, shards(): fit_rhs = lax.psum(partial_value, 'pix') / npix  26.7 us
    dot_general x1, matrix products, shards(): local_gram = jnp.dot(centered, centered.T, precision=lax.Precision.HIGHEST)  17.3 us
    all_to_all x1, other arithmetic, shards(): lax.all_to_all(tiles_out, 'pix', split_axis=2, concat_axis=1, tiled=True)  13.7 us
    all_to_all x2, local copies, waits for them, and re-layouts, shards(): lax.all_to_all(tiles_out, 'pix', split_axis=2, concat_axis=1, tiled=True)  12.5 us
  transfers between devices with their start and end apart: 3, of which 2 were waited for; matrix products, arithmetic and copies ran while one was open for 11% of the time, Pallas kernels for 0%

commit v1 on v0

v1 whole, which is shorter than its diff:
```python
import functools

import jax
import jax.numpy as jnp
from jax import lax
from jax.experimental import pallas as pl
from jax.experimental.pallas import tpu as pltpu
from jax.sharding import PartitionSpec as P

SUBSPACE = 2
MESH = pl.DeviceIdType.MESH
HIGHEST = lax.Precision.HIGHEST
VMEM_LIMIT = 56 * 1024 * 1024

floor_value = 0.2


def dot_nt(a, b, precision=None):
    return lax.dot_general(
        a, b, (((1,), (1,)), ((), ())), precision=precision, preferred_element_type=jnp.float32
    )


def split(x):
    high = x.astype(jnp.bfloat16)
    low = (x - high.astype(jnp.float32)).astype(jnp.bfloat16)
    return high, low


def greet(ang, pix, a, p):
    barrier = pltpu.get_barrier_semaphore()
    for d in range(1, ang):
        pl.semaphore_signal(
            barrier, inc=1, device_id=(lax.rem(a + d, ang), p), device_id_type=MESH
        )
    for e in range(1, pix):
        pl.semaphore_signal(
            barrier, inc=1, device_id=(a, lax.rem(p + e, pix)), device_id_type=MESH
        )


def await_greetings(ang, pix):
    pl.semaphore_wait(pltpu.get_barrier_semaphore(), ang + pix - 2)


def send(src, dst, send_sem, recv_sem, device):
    copy = pltpu.make_async_remote_copy(
        src_ref=src, dst_ref=dst, send_sem=send_sem, recv_sem=recv_sem,
        device_id=device, device_id_type=MESH,
    )
    copy.start()
    return copy


LANES = 128


def load_strips(source, target, sems):
    copies = []
    for c in range(target.shape[0]):
        copy = pltpu.make_async_copy(
            source.at[:, pl.ds(c * LANES, LANES)], target.at[c], sems.at[c]
        )
        copy.start()
        copies.append(copy)
    return copies


def strided_row(strips, first, count, stride, group):
    return jnp.concatenate(
        [strips[c, pl.ds(first, count, stride=stride), :] for c in group], axis=1
    )


def gram_kernel(ang, pix, frames, rows, reduce_here, flats, gram, x, acc, cross, total,
                from_ang, from_pix, load_sem, s1, r1, s2, r2, s3, r3, s4, r4):
    a, p = lax.axis_index("ang"), lax.axis_index("pix")
    if reduce_here:
        greet(ang, pix, a, p)
    copies = load_strips(flats, x, load_sem)
    acc[...] = jnp.zeros_like(acc)
    cross[...] = jnp.zeros_like(cross)
    for c in range(0, len(copies), 2):
        copies[c].wait()
        copies[c + 1].wait()

        def one_row(r, carry):
            here = strided_row(x, r, frames, rows, (c, c + 1))
            high, low = split(here - jnp.mean(here, axis=0, keepdims=True))
            acc[...] += dot_nt(high, high)
            cross[...] += dot_nt(high, low)
            return carry
        lax.fori_loop(0, rows, one_row, 0)
    both = cross[...]
    acc[...] += both + both.T
    if not reduce_here:
        gram[...] = acc[...]
        return
    await_greetings(ang, pix)
    block = frames // ang
    piece = block // pix
    first = []
    for d in range(1, ang):
        x_to = lax.rem(a + d, ang)
        first.append(send(acc.at[pl.ds(pl.multiple_of(x_to * block, block), block)],
                          from_ang.at[d], s1.at[d], r1.at[d], (x_to, p)))
    mine = acc[pl.ds(pl.multiple_of(a * block, block), block), :]
    for copy in first:
        copy.wait_recv()
    for d in range(1, ang):
        mine = mine + from_ang[d]
    from_ang[0] = mine
    second = []
    for e in range(1, pix):
        q = lax.rem(p + e, pix)
        second.append(send(from_ang.at[0, pl.ds(pl.multiple_of(q * piece, piece), piece)],
                           from_pix.at[e], s2.at[e], r2.at[e], (a, q)))
    own = from_ang[0, pl.ds(pl.multiple_of(p * piece, piece), piece), :]
    for copy in second:
        copy.wait_recv()
    for e in range(1, pix):
        own = own + from_pix[e]
    at = pl.ds(pl.multiple_of(a * block + p * piece, piece), piece)
    total[at, :] = own
    third = []
    for e in range(1, pix):
        q = lax.rem(p + e, pix)
        third.append(send(total.at[at], total.at[at], s3.at[e], r3.at[e], (a, q)))
    for copy in third:
        copy.wait_recv()
    at = pl.ds(pl.multiple_of(a * block, block), block)
    fourth = []
    for d in range(1, ang):
        x_to = lax.rem(a + d, ang)
        fourth.append(send(total.at[at], total.at[at], s4.at[d], r4.at[d], (x_to, p)))
    for copy in fourth:
        copy.wait_recv()
    gram[...] = total[...]
    for copy in first + second + third + fourth:
        copy.wait_send()


def gram_of(flats, ang, pix):
    frames, rows, cols = flats.shape
    reduce_here = frames % (ang * pix * 8) == 0
    block, piece = frames // ang, max(8, frames // ang // pix)
    vmem, dma = pltpu.VMEM, pltpu.SemaphoreType.DMA
    gram = pl.pallas_call(
        functools.partial(gram_kernel, ang, pix, frames, rows, reduce_here),
        out_shape=jax.ShapeDtypeStruct((frames, frames), jnp.float32),
        in_specs=[pl.BlockSpec(memory_space=pl.ANY)],
        out_specs=pl.BlockSpec(memory_space=vmem),
        scratch_shapes=[
            vmem((cols // LANES, frames * rows, LANES), jnp.float32),
            vmem((frames, frames), jnp.float32),
            vmem((frames, frames), jnp.float32),
            vmem((frames, frames), jnp.float32),
            vmem((ang, block, frames), jnp.float32),
            vmem((pix, piece, frames), jnp.float32),
            dma((cols // LANES,)),
            dma((ang,)), dma((ang,)), dma((pix,)), dma((pix,)),
            dma((pix,)), dma((pix,)), dma((ang,)), dma((ang,)),
        ],
        compiler_params=pltpu.CompilerParams(
            collective_id=0 if reduce_here else None,
            has_side_effects=reduce_here, vmem_limit_bytes=VMEM_LIMIT,
        ),
        name="gram",
    )(flats.reshape(frames * rows, cols))
    return gram if reduce_here else lax.psum(gram, ("ang", "pix"))


def correct_kernel(ang, pix, frames, rows, angles, all_rows, modes, npix,
                   flats, projections, basis_t, solver, out,
                   x, proj, done, e_own, e_rows, e_all, fit, part, parts,
                   load_sem, proj_sem, out_sem, keep_sem, s1, r1, s2, r2, s3, r3, s4, r4):
    a, p = lax.axis_index("ang"), lax.axis_index("pix")
    greet(ang, pix, a, p)
    copies = load_strips(flats, x, load_sem)
    proj_copies = load_strips(projections, proj, proj_sem)
    quarter = rows // ang
    strips = proj.shape[0]
    wide = strips * LANES
    share = pix // ang
    e_own[...] = jnp.zeros_like(e_own)
    fit[...] = jnp.zeros_like(fit)
    b_high, b_low = split(basis_t[...])
    b_both = jnp.concatenate([b_high, b_low], axis=0)
    for copy in copies:
        copy.wait()

    def eigen_rows(x_to):
        for c in range(0, len(copies), 2):
            cut = pl.ds(c * LANES, 2 * LANES)
            for i in range(quarter):
                here = strided_row(x, x_to * quarter + i, frames, rows, (c, c + 1))
                mean = jnp.mean(here, axis=0, keepdims=True)
                high, low = split(here - mean)
                one = jnp.dot(b_both, high, preferred_element_type=jnp.float32)
                two = jnp.dot(b_high, low, preferred_element_type=jnp.float32)
                e_own[x_to, i * modes:(i + 1) * modes, cut] = one[:modes] + one[modes:] + two
                e_own[x_to, quarter * modes + i:quarter * modes + i + 1, cut] = mean

    first = []
    for d in range(1, ang):
        x_to = lax.rem(a + d, ang)
        eigen_rows(x_to)
        if d == 1:
            await_greetings(ang, pix)
        first.append(send(e_own.at[x_to], e_rows.at[a], s1.at[d], r1.at[d], (x_to, p)))
    eigen_rows(a)
    e_rows[a] = e_own[a]
    for copy in proj_copies:
        copy.wait()
    for copy in first:
        copy.wait_recv()

    def cut_for(q):
        return e_rows.at[q // share, :, pl.ds(pl.multiple_of(lax.rem(q, share) * wide, wide), wide)]

    keep = pltpu.make_async_copy(cut_for(p), e_all.at[a, p], keep_sem)
    keep.start()
    second = []
    for e in range(1, pix):
        q = lax.rem(p + e, pix)
        second.append(send(cut_for(q), e_all.at[a, p], s2.at[e], r2.at[e], (a, q)))
    keep.wait()

    def add_fit(x_at, q):
        for i in range(quarter):
            row = q * rows + x_at * quarter + i
            mean = e_all[x_at, q, quarter * modes + i:quarter * modes + i + 1, :]
            here = strided_row(proj, row, angles, all_rows, range(strips)) - mean
            eigen = e_all[x_at, q, i * modes:(i + 1) * modes, :]
            left = jnp.concatenate(split(here), axis=0)
            right = jnp.concatenate(split(eigen), axis=0)
            fit[...] += dot_nt(left, right)

    third = []
    for e in range(pix):
        q = lax.rem(p + pix - e, pix)
        if e:
            second[e - 1].wait_recv()
        for d in range(1, ang):
            third.append(send(e_all.at[a, q], e_all.at[a, q], s3.at[d, e], r3.at[d, e],
                              (lax.rem(a + d, ang), p)))
        add_fit(a, q)
    for e in range(pix):
        q = lax.rem(p + pix - e, pix)
        for d in range(1, ang):
            third[e * (ang - 1) + d - 1].wait_recv()
            add_fit(lax.rem(a + ang - d, ang), q)
    sums = fit[...]
    part[...] = jnp.zeros_like(part)
    part[:, :modes] = (sums[:angles, :modes] + sums[:angles, modes:]
                       + sums[angles:, :modes] + sums[angles:, modes:])
    fourth = []
    for e in range(1, pix):
        fourth.append(send(part, parts.at[e], s4.at[e], r4.at[e], (a, lax.rem(p + e, pix))))
    whole = part[...]
    for copy in fourth:
        copy.wait_recv()
    for e in range(1, pix):
        whole = whole + parts[e]
    fit_rhs = whole[:, :modes] / npix
    inner = dot_nt(fit_rhs, solver[...], HIGHEST)
    weights = jnp.dot(inner, solver[...], precision=HIGHEST, preferred_element_type=jnp.float32)
    w_high, w_low = split(weights)
    w_all = jnp.concatenate([w_high, w_low, w_high], axis=1)

    def finish(q, carry):
        for x_at in range(ang):
            for i in range(quarter):
                row = q * rows + x_at * quarter + i
                mean = e_all[x_at, q, quarter * modes + i:quarter * modes + i + 1, :]
                e_high, e_low = split(e_all[x_at, q, i * modes:(i + 1) * modes, :])
                e_cat = jnp.concatenate([e_high, e_high, e_low], axis=0)
                estimate = mean + jnp.dot(w_all, e_cat, preferred_element_type=jnp.float32)
                floored = jnp.maximum(estimate, floor_value)
                at = pl.ds(row, angles, stride=all_rows)
                for c in range(strips):
                    done[c, at, :] = proj[c, at, :] / floored[:, c * LANES:(c + 1) * LANES]
        return carry
    lax.fori_loop(0, pix, finish, 0)
    out_copies = []
    for c in range(strips):
        copy = pltpu.make_async_copy(done.at[c], out.at[:, pl.ds(c * LANES, LANES)], out_sem.at[c])
        copy.start()
        out_copies.append(copy)
    for copy in out_copies:
        copy.wait()
    for copy in first + second + third + fourth:
        copy.wait_send()


def correct(flats, projections, basis_t, solver, ang, pix, npix):
    frames, rows, cols = flats.shape
    angles, all_rows, wide = projections.shape
    modes = basis_t.shape[0]
    unit = (rows // ang) * modes + 8
    vmem, dma = pltpu.VMEM, pltpu.SemaphoreType.DMA
    out = pl.pallas_call(
        functools.partial(correct_kernel, ang, pix, frames, rows, angles, all_rows, modes, npix),
        out_shape=jax.ShapeDtypeStruct((angles * all_rows, wide), jnp.float32),
        in_specs=[pl.BlockSpec(memory_space=pl.ANY)] * 2 + [pl.BlockSpec(memory_space=vmem)] * 2,
        out_specs=pl.BlockSpec(memory_space=pl.ANY),
        scratch_shapes=[
            vmem((cols // LANES, frames * rows, LANES), jnp.float32),
            vmem((wide // LANES, angles * all_rows, LANES), jnp.float32),
            vmem((wide // LANES, angles * all_rows, LANES), jnp.float32),
            vmem((ang, unit, cols), jnp.float32),
            vmem((ang, unit, cols), jnp.float32),
            vmem((ang, pix, unit, wide), jnp.float32),
            vmem((2 * angles, 2 * modes), jnp.float32),
            vmem((angles, 128), jnp.float32),
            vmem((pix, angles, 128), jnp.float32),
            dma((cols // LANES,)), dma((wide // LANES,)), dma((wide // LANES,)), dma,
            dma((ang,)), dma((ang,)), dma((pix,)), dma((pix,)),
            dma((ang, pix)), dma((ang, pix)), dma((pix,)), dma((pix,)),
        ],
        compiler_params=pltpu.CompilerParams(
            collective_id=1, has_side_effects=True, vmem_limit_bytes=VMEM_LIMIT
        ),
        name="correct",
    )(flats.reshape(frames * rows, cols), projections.reshape(angles * all_rows, wide),
      basis_t, solver)
    return out.reshape(projections.shape)


def orthonormal(grown):
    correlation = jnp.dot(grown.T, grown, precision=HIGHEST)
    lower = jnp.linalg.cholesky(correlation)
    return jax.scipy.linalg.solve_triangular(lower, grown.T, lower=True).T


def shards(flats, projections, start_basis):
    rows_dev, cols_dev = flats.shape[1:]
    ang, pix = lax.axis_size("ang"), lax.axis_size("pix")
    npix = rows_dev * cols_dev * ang * pix
    gram = gram_of(flats, ang, pix) / npix
    basis = start_basis
    for turn in range(SUBSPACE):
        basis = orthonormal(jnp.dot(gram, basis, precision=HIGHEST))
    normal = jnp.dot(basis.T, jnp.dot(gram, basis, precision=HIGHEST), precision=HIGHEST)
    factor = jnp.linalg.cholesky(normal)
    solver = jax.scipy.linalg.solve_triangular(
        factor, jnp.eye(factor.shape[0], dtype=jnp.float32), lower=True
    )
    return correct(flats, projections, basis.T, solver, ang, pix, npix)


def solution(mesh):
    in_specs = (P(None, "pix", "ang"), P("ang", None, "pix"), P())
    out_specs = P("ang", None, "pix")
    return jax.shard_map(shards, mesh=mesh, in_specs=in_specs, out_specs=out_specs, check_vma=False)
```

time: 550 us -> 194 us (0.35); the launches traced: 540 us -> 194 us
  waiting for transfers between devices: 177 us -> 0 us
  Pallas kernels: 0 us -> 154 us
  blocking collectives: 135 us -> 0 us
  local copies, waits for them, and re-layouts: 108 us -> 5.14 us
  matrix products: 45.5 us -> 5.81 us
  other arithmetic: 54.9 us -> 28.3 us
  between operations: 13.8 us -> 0.16 us
    pallas_call x0 -> x2, Pallas kernels: none -> 154 us  [the longest x1 120 us: correct(): pl.pallas_call(functools.partial(correct_kernel, ang, pix, frames, rows,...]
    psum x1 -> x0, waiting for transfers between devices: 103 us -> none  [shards(): gram = lax.psum(local_gram, ('ang', 'pix')) / npix]
    all_to_all x1 -> x0, blocking collectives: 98.7 us -> none  [shards(): lax.all_to_all(tiles_out, 'pix', split_axis=2, concat_axis=1, tiled=True)]
    all_to_all x1 -> x0, waiting for transfers between devices: 74.3 us -> none  [shards(): lax.all_to_all(projections, 'pix', split_axis=1, concat_axis=2, tiled=True)]
    unnamed x20 -> x5, local copies, waits for them, and re-layouts: 67.5 us -> 4.93 us
    dot_general x10 -> x6, matrix products: 44.7 us -> 4.49 us  [the longest x2 2.61 us: shards(): basis = orthonormal(jnp.dot(gram, basis, precision=HIGHEST))]
    psum x1 -> x0, blocking collectives: 26.7 us -> none  [shards(): fit_rhs = lax.psum(partial_value, 'pix') / npix]
    all_to_all x3 -> x0, local copies, waits for them, and re-layouts: 17.1 us -> none  [the longest x2 12.5 us: shards(): lax.all_to_all(tiles_out, 'pix', split_axis=2, concat_axis=1, tiled=True)]
  transfers between devices with their start and end apart: 3 -> 0, of which waited for: 2 -> 0; matrix products, arithmetic and copies ran while one was open for 11% -> 0% of each run, Pallas kernels for 0% -> 0%
where the time goes in v1:
time: 194 us
  Pallas kernels  154 us (79%)
  other arithmetic  28.3 us (15%)
  matrix products  5.81 us (3%)
  local copies, waits for them, and re-layouts  5.14 us (3%)
    pallas_call x1, Pallas kernels, correct(): pl.pallas_call(functools.partial(correct_kernel, ang, pix, frames, rows,...  120 us
    pallas_call x1, Pallas kernels, gram_of(): pl.pallas_call(functools.partial(gram_kernel, ang, pix, frames, rows, red...  34.2 us
    another operation x6, other arithmetic, orthonormal(): lower = jnp.linalg.cholesky(correlation)  10.1 us
    another operation x4, other arithmetic, orthonormal(): return jax.scipy.linalg.solve_triangular(lower, grown.T, lower=True).T  8.65 us
    another operation x3, other arithmetic, shards(): factor = jnp.linalg.cholesky(normal)  5.13 us
    unnamed x5, local copies, waits for them, and re-layouts  4.93 us
    another operation x2, other arithmetic, shards(): jax.scipy.linalg.solve_triangular(factor, jnp.eye(factor.shape[0], dtype=...  4.37 us

profile of v1, /device:TPU:0, one launch (start us, length us, event | category | flops | bytes accessed | tf_op | source)
XLA Modules:
  0.0 193.7 jit_solution(15585174209411044691)
XLA Ops:
  0.0 0.0 copy-start
  0.0 34.2 %gram.1 = f32[256,256]{1,0:T(8,128)} custom-call(f32[2048,1024]{1,0:T(8,128)} %bitcast.45), custom_call_target="tpu_custom_call" | custom-call | tf_op jit(solution)/shard_map/gram/pallas_call | solution.py:148
  34.2 0.0 copy-done
  34.2 1.3 fusion.4
  35.5 0.2 fusion.28
  35.7 0.1 copy.4
  35.8 4.4 %cholesky.59 = f32[48,48]{1,0:T(8,128)S(1)} custom-call(f32[48,48]{1,0:T(8,128)S(1)} %fusion.22), custom_call_target="Cholesky" | custom-call | tf_op jit(solution)/shard_map/jit(cholesky)/cholesky | solution.py:332
  40.2 0.6 compare_reduce_fusion.2
  40.9 0.7 fusion.13
  41.6 3.7 %custom-call.11 = f32[1,48,48]{1,2,0:T(8,128)S(1)} custom-call(f32[1,48,48]{2,1,0:T(8,128)S(1)} %fusion.13), custom_call_target="InvertDiagBlocksLowerTriangular" | custom-call | tf_op jit(solution)/shard_map/jit(_solve_triangular)/triangular_solve | solution.py:333
  45.2 0.2 fusion.11
  45.5 1.3 fusion.2
  46.8 0.2 fusion.29
  47.0 0.1 copy.5
  47.1 4.4 %cholesky.70 = f32[48,48]{1,0:T(8,128)S(1)} custom-call(f32[48,48]{1,0:T(8,128)S(1)} %fusion.20), custom_call_target="Cholesky" | custom-call | tf_op jit(solution)/shard_map/jit(cholesky)/cholesky | solution.py:332
  51.5 0.6 compare_reduce_fusion.1
  52.1 0.7 fusion.14
  52.8 3.7 %custom-call.12 = f32[1,48,48]{1,2,0:T(8,128)S(1)} custom-call(f32[1,48,48]{2,1,0:T(8,128)S(1)} %fusion.14), custom_call_target="InvertDiagBlocksLowerTriangular" | custom-call | tf_op jit(solution)/shard_map/jit(_solve_triangular)/triangular_solve | solution.py:333
  56.5 0.2 fusion.9.basis_t
  56.7 0.0 copy-start.1
  56.7 1.3 fusion
  58.1 0.2 fusion.30
  58.3 0.1 copy.6
  58.4 4.4 %cholesky.81 = f32[48,48]{1,0:T(8,128)S(1)} custom-call(f32[48,48]{1,0:T(8,128)S(1)} %fusion.18), custom_call_target="Cholesky" | custom-call | tf_op jit(solution)/shard_map/jit(cholesky)/cholesky | solution.py:345
  62.8 0.7 compare_reduce_fusion
  63.5 0.7 fusion.15
  64.2 3.7 %custom-call.9 = f32[1,48,48]{1,2,0:T(8,128)S(1)} custom-call(f32[1,48,48]{2,1,0:T(8,128)S(1)} %fusion.15), custom_call_target="InvertDiagBlocksLowerTriangular" | custom-call | tf_op jit(solution)/shard_map/jit(_solve_triangular)/triangular_solve | solution.py:346
  67.9 0.8 fusion.16.solver
  68.7 0.0 copy-done.1
  68.7 120.1 %correct.1 = f32[2048,512]{1,0:T(8,128)} custom-call(f32[2048,1024]{1,0:T(8,128)} %bitcast.46, f32[2048,512]{1,0:T(8,128)} %bitcast.48, f32[48,256]{1,0:T(8,128)} %copy-done.1, f32[48,48]{1,0:T(8,128)} %fusion.16.solver), custom_call_target="tpu_custom_call" | custom-call | tf_op jit(solution)/shard_map/correct/pallas_call | solution.py:302
  188.8 4.9 %copy.8 = f32[32,64,512]{2,1,0:T(8,128)} copy(f32[32,64,512]{2,1,0:T(8,128)} %bitcast.47) | data formatting | bytes 8388608
  (6 shorter events, 0.1 us)
Async XLA Ops:
  0.0 34.2 %copy-start = (f32[256,48]{0,1:T(8,128)S(1)}, f32[256,48]{0,1:T(8,128)}, u32[]{:S(2)}) copy-start(f32[256,48]{0,1:T(8,128)} %param.8) | copy-start | bytes 147460
  56.7 12.0 %copy-start.1 = (f32[48,256]{1,0:T(8,128)}, f32[48,256]{1,0:T(8,128)S(1)}, u32[]{:S(2)}) copy-start(f32[48,256]{1,0:T(8,128)S(1)} %fusion.9.basis_t) | copy-start | bytes 147460

commit v2 on v1

--- a/solution.py
+++ b/solution.py
@@ -170,10 +170,10 @@
     return gram if reduce_here else lax.psum(gram, ("ang", "pix"))
 
 
-def correct_kernel(ang, pix, frames, rows, angles, all_rows, modes, npix,
-                   flats, projections, basis_t, solver, out,
-                   x, proj, done, e_own, e_rows, e_all, fit, part, parts,
-                   load_sem, proj_sem, out_sem, keep_sem, s1, r1, s2, r2, s3, r3, s4, r4):
+def fit_kernel(ang, pix, frames, rows, angles, all_rows, modes, npix,
+                   flats, projections, basis_t, solver, eigen_out, weights_out,
+                   x, proj, e_own, e_rows, e_all, fit, part, parts,
+                   load_sem, proj_sem, store_sem, keep_sem, s1, r1, s2, r2, s3, r3, s4, r4):
     a, p = lax.axis_index("ang"), lax.axis_index("pix")
     greet(ang, pix, a, p)
     copies = load_strips(flats, x, load_sem)
@@ -236,20 +236,45 @@
             right = jnp.concatenate(split(eigen), axis=0)
             fit[...] += dot_nt(left, right)
 
-    third = []
-    for e in range(pix):
-        q = lax.rem(p + pix - e, pix)
+    across = a + 1 - 2 * lax.rem(a, 2)
+    along = lax.rem(a + 2, ang)
+    corner = lax.rem(across + 2, ang)
+    top = e_all.shape[2] // 16 * 8
+    bottom = e_all.shape[2] - top
+    to_across, to_along, on_top, on_bottom, stores = [], [], [], [], []
+
+    def pass_on(e, q):
         if e:
             second[e - 1].wait_recv()
-        for d in range(1, ang):
-            third.append(send(e_all.at[a, q], e_all.at[a, q], s3.at[d, e], r3.at[d, e],
-                              (lax.rem(a + d, ang), p)))
+        piece = e_all.at[a, q]
+        to_across.append(send(piece, piece, s3.at[0, e], r3.at[0, e], (across, p)))
+        to_along.append(send(piece, piece, s3.at[1, e], r3.at[1, e], (along, p)))
         add_fit(a, q)
-    for e in range(pix):
-        q = lax.rem(p + pix - e, pix)
-        for d in range(1, ang):
-            third[e * (ang - 1) + d - 1].wait_recv()
-            add_fit(lax.rem(a + ang - d, ang), q)
+
+    def forward(e, q):
+        to_across[e].wait_recv()
+        piece = e_all.at[across, q, pl.ds(0, top)]
+        on_top.append(send(piece, piece, s3.at[2, e], r3.at[2, e], (along, p)))
+        to_along[e].wait_recv()
+        piece = e_all.at[along, q, pl.ds(top, bottom)]
+        on_bottom.append(send(piece, piece, s3.at[3, e], r3.at[3, e], (across, p)))
+        add_fit(across, q)
+        add_fit(along, q)
+
+    def complete(e, q):
+        on_top[e].wait_recv()
+        on_bottom[e].wait_recv()
+        copy = pltpu.make_async_copy(e_all.at[:, q], eigen_out.at[:, q], store_sem.at[e])
+        copy.start()
+        stores.append(copy)
+        add_fit(corner, q)
+
+    for step in range(pix + 2):
+        for lag, stage in enumerate((pass_on, forward, complete)):
+            e = step - lag
+            if 0 <= e < pix:
+                stage(e, lax.rem(p + pix - e, pix))
+    third = to_across + to_along + on_top + on_bottom
     sums = fit[...]
     part[...] = jnp.zeros_like(part)
     part[:, :modes] = (sums[:angles, :modes] + sums[:angles, modes:]
@@ -265,88 +290,142 @@
     fit_rhs = whole[:, :modes] / npix
     inner = dot_nt(fit_rhs, solver[...], HIGHEST)
     weights = jnp.dot(inner, solver[...], precision=HIGHEST, preferred_element_type=jnp.float32)
-    w_high, w_low = split(weights)
-    w_all = jnp.concatenate([w_high, w_low, w_high], axis=1)
-
-    def finish(q, carry):
-        for x_at in range(ang):
-            for i in range(quarter):
-                row = q * rows + x_at * quarter + i
-                mean = e_all[x_at, q, quarter * modes + i:quarter * modes + i + 1, :]
-                e_high, e_low = split(e_all[x_at, q, i * modes:(i + 1) * modes, :])
-                e_cat = jnp.concatenate([e_high, e_high, e_low], axis=0)
-                estimate = mean + jnp.dot(w_all, e_cat, preferred_element_type=jnp.float32)
-                floored = jnp.maximum(estimate, floor_value)
-                at = pl.ds(row, angles, stride=all_rows)
-                for c in range(strips):
-                    done[c, at, :] = proj[c, at, :] / floored[:, c * LANES:(c + 1) * LANES]
-        return carry
-    lax.fori_loop(0, pix, finish, 0)
-    out_copies = []
-    for c in range(strips):
-        copy = pltpu.make_async_copy(done.at[c], out.at[:, pl.ds(c * LANES, LANES)], out_sem.at[c])
-        copy.start()
-        out_copies.append(copy)
-    for copy in out_copies:
+    weights_out[...] = jnp.zeros_like(weights_out)
+    weights_out[:, :modes] = weights
+    for copy in stores:
         copy.wait()
     for copy in first + second + third + fourth:
         copy.wait_send()
 
 
-def correct(flats, projections, basis_t, solver, ang, pix, npix):
+def fit_weights(flats, projections, basis_t, solver, ang, pix, npix):
     frames, rows, cols = flats.shape
     angles, all_rows, wide = projections.shape
     modes = basis_t.shape[0]
     unit = (rows // ang) * modes + 8
     vmem, dma = pltpu.VMEM, pltpu.SemaphoreType.DMA
-    out = pl.pallas_call(
-        functools.partial(correct_kernel, ang, pix, frames, rows, angles, all_rows, modes, npix),
-        out_shape=jax.ShapeDtypeStruct((angles * all_rows, wide), jnp.float32),
+    return pl.pallas_call(
+        functools.partial(fit_kernel, ang, pix, frames, rows, angles, all_rows, modes, npix),
+        out_shape=(
+            jax.ShapeDtypeStruct((ang, pix, unit, wide), jnp.float32),
+            jax.ShapeDtypeStruct((angles, LANES), jnp.float32),
+        ),
         in_specs=[pl.BlockSpec(memory_space=pl.ANY)] * 2 + [pl.BlockSpec(memory_space=vmem)] * 2,
-        out_specs=pl.BlockSpec(memory_space=pl.ANY),
+        out_specs=(pl.BlockSpec(memory_space=pl.ANY), pl.BlockSpec(memory_space=vmem)),
         scratch_shapes=[
             vmem((cols // LANES, frames * rows, LANES), jnp.float32),
-            vmem((wide // LANES, angles * all_rows, LANES), jnp.float32),
             vmem((wide // LANES, angles * all_rows, LANES), jnp.float32),
             vmem((ang, unit, cols), jnp.float32),
             vmem((ang, unit, cols), jnp.float32),
             vmem((ang, pix, unit, wide), jnp.float32),
             vmem((2 * angles, 2 * modes), jnp.float32),
-            vmem((angles, 128), jnp.float32),
-            vmem((pix, angles, 128), jnp.float32),
-            dma((cols // LANES,)), dma((wide // LANES,)), dma((wide // LANES,)), dma,
+            vmem((angles, LANES), jnp.float32),
+            vmem((pix, angles, LANES), jnp.float32),
+            dma((cols // LANES,)), dma((wide // LANES,)), dma((pix,)), dma,
             dma((ang,)), dma((ang,)), dma((pix,)), dma((pix,)),
-            dma((ang, pix)), dma((ang, pix)), dma((pix,)), dma((pix,)),
+            dma((4, pix)), dma((4, pix)), dma((pix,)), dma((pix,)),
         ],
         compiler_params=pltpu.CompilerParams(
             collective_id=1, has_side_effects=True, vmem_limit_bytes=VMEM_LIMIT
         ),
-        name="correct",
+        name="fit",
     )(flats.reshape(frames * rows, cols), projections.reshape(angles * all_rows, wide),
       basis_t, solver)
+
+
+def correct_kernel(ang, pix, rows, modes, proj, eigen, weights, out):
+    angles = weights.shape[0]
+    all_rows = proj.shape[0] // angles
+    quarter = rows // ang
+    w_high, w_low = split(weights[:, :modes])
+    w_all = jnp.concatenate([w_high, w_low, w_high], axis=1)
+
+    def finish(q, carry):
+        for x_at in range(ang):
+            for i in range(quarter):
+                mean = eigen[x_at, q, quarter * modes + i:quarter * modes + i + 1, :]
+                e_high, e_low = split(eigen[x_at, q, i * modes:(i + 1) * modes, :])
+                e_cat = jnp.concatenate([e_high, e_high, e_low], axis=0)
+                estimate = mean + jnp.dot(w_all, e_cat, preferred_element_type=jnp.float32)
+                at = pl.ds(q * rows + x_at * quarter + i, angles, stride=all_rows)
+                out[at, :] = proj[at, :] / jnp.maximum(estimate, floor_value)
+        return carry
+    lax.fori_loop(0, pix, finish, 0)
+
+
+def correct(projections, eigen, weights, rows, modes):
+    angles, all_rows, wide = projections.shape
+    ang, pix, unit, _ = eigen.shape
+    strip = pl.BlockSpec((angles * all_rows, LANES), lambda c: (0, c))
+    out = pl.pallas_call(
+        functools.partial(correct_kernel, ang, pix, rows, modes),
+        grid=(wide // LANES,),
+        out_shape=jax.ShapeDtypeStruct((angles * all_rows, wide), jnp.float32),
+        in_specs=[
+            strip,
+            pl.BlockSpec((ang, pix, unit, LANES), lambda c: (0, 0, 0, c)),
+            pl.BlockSpec((angles, LANES), lambda c: (0, 0)),
+        ],
+        out_specs=strip,
+        compiler_params=pltpu.CompilerParams(vmem_limit_bytes=VMEM_LIMIT),
+        name="correct",
+    )(projections.reshape(angles * all_rows, wide), eigen, weights)
     return out.reshape(projections.shape)
 
 
-def orthonormal(grown):
-    correlation = jnp.dot(grown.T, grown, precision=HIGHEST)
-    lower = jnp.linalg.cholesky(correlation)
-    return jax.scipy.linalg.solve_triangular(lower, grown.T, lower=True).T
+def inverse_factor(matrix):
+    order = matrix.shape[0]
+    side = 64
+    place = lax.broadcasted_iota(jnp.int32, (order, order), 0)
+    other = lax.broadcasted_iota(jnp.int32, (order, order), 1)
+    unit = (place == other).astype(jnp.float32)
+    gap = jnp.zeros((order, side - order), jnp.float32)
+    table = jnp.concatenate([matrix, gap, unit, gap], axis=1)
+    below = lax.broadcasted_iota(jnp.int32, (order, 1), 0)
+    for j in range(order - 1):
+        row = table[j:j + 1, :]
+        factor = table[:, j:j + 1] / table[j:j + 1, j:j + 1]
+        table = table - jnp.where(below > j, factor, 0.0) * row
+    pivots = jnp.sum(table[:, :order] * unit, axis=1, keepdims=True)
+    return table[:, side:side + order] / jnp.sqrt(pivots)
+
+
+def dot_exact(a, b):
+    return jnp.dot(a, b, precision=HIGHEST, preferred_element_type=jnp.float32)
+
+
+def basis_kernel(npix, gram_ref, start, basis_t, solver):
+    gram = gram_ref[...] / npix
+    basis = start[...]
+    for turn in range(SUBSPACE):
+        grown = dot_exact(basis, gram)
+        basis = dot_exact(inverse_factor(dot_nt(grown, grown, HIGHEST)), grown)
+    basis_t[...] = basis
+    normal = dot_nt(dot_exact(basis, gram), basis, HIGHEST)
+    solver[...] = inverse_factor(normal)
+
+
+def basis_of(gram, start_basis, npix):
+    modes = start_basis.shape[1]
+    return pl.pallas_call(
+        functools.partial(basis_kernel, npix),
+        out_shape=(
+            jax.ShapeDtypeStruct(start_basis.shape[::-1], jnp.float32),
+            jax.ShapeDtypeStruct((modes, modes), jnp.float32),
+        ),
+        compiler_params=pltpu.CompilerParams(vmem_limit_bytes=VMEM_LIMIT),
+        name="basis",
+    )(gram, start_basis.T)
 
 
 def shards(flats, projections, start_basis):
     rows_dev, cols_dev = flats.shape[1:]
     ang, pix = lax.axis_size("ang"), lax.axis_size("pix")
     npix = rows_dev * cols_dev * ang * pix
-    gram = gram_of(flats, ang, pix) / npix
-    basis = start_basis
-    for turn in range(SUBSPACE):
-        basis = orthonormal(jnp.dot(gram, basis, precision=HIGHEST))
-    normal = jnp.dot(basis.T, jnp.dot(gram, basis, precision=HIGHEST), precision=HIGHEST)
-    factor = jnp.linalg.cholesky(normal)
-    solver = jax.scipy.linalg.solve_triangular(
-        factor, jnp.eye(factor.shape[0], dtype=jnp.float32), lower=True
-    )
-    return correct(flats, projections, basis.T, solver, ang, pix, npix)
+    gram = gram_of(flats, ang, pix)
+    basis_t, solver = basis_of(gram, start_basis, npix)
+    eigen, weights = fit_weights(flats, projections, basis_t, solver, ang, pix, npix)
+    return correct(projections, eigen, weights, rows_dev, basis_t.shape[0])
 
 
 def solution(mesh):

time: 194 us -> 165 us (0.85)
  other arithmetic: 28.3 us -> 0 us
  Pallas kernels: 154 us -> 164 us
  matrix products: 5.81 us -> 0 us
  local copies, waits for them, and re-layouts: 5.14 us -> 0 us
    another operation x15 -> x0, other arithmetic: 28.3 us -> none  [the longest x6 10.1 us: orthonormal(): lower = jnp.linalg.cholesky(correlation)]
    pallas_call x1 -> x3, Pallas kernels: 120 us -> 130 us  [the longest x1 103 us: fit_weights(): pl.pallas_call(functools.partial(fit_kernel, ang, pix, frames, rows, angl...]
    unnamed x5 -> x0, local copies, waits for them, and re-layouts: 4.93 us -> none
    dot_general x6 -> x0, matrix products: 4.49 us -> none  [the longest x2 2.61 us: shards(): basis = orthonormal(jnp.dot(gram, basis, precision=HIGHEST))]
where the time goes in v2:
time: 165 us; the launch traced here: 164 us
  Pallas kernels  164 us (99%)
    pallas_call x1, Pallas kernels, fit_weights(): pl.pallas_call(functools.partial(fit_kernel, ang, pix, frames, rows, angl...  103 us
    pallas_call x1, Pallas kernels, gram_of(): pl.pallas_call(functools.partial(gram_kernel, ang, pix, frames, rows, red...  34.2 us
    pallas_call x1, Pallas kernels, basis_of(): pl.pallas_call(functools.partial(basis_kernel, npix), out_shape=(jax.Shap...  15.4 us
    pallas_call x1, Pallas kernels, correct(): pl.pallas_call(functools.partial(correct_kernel, ang, pix, rows, modes),...  12.4 us

profile of v2, /device:TPU:0, one launch (start us, length us, event | category | flops | bytes accessed | tf_op | source)
XLA Modules:
  0.0 164.5 jit_solution(7091469083767859848)
XLA Ops:
  0.0 34.2 %gram.1.gram_ref = f32[256,256]{1,0:T(8,128)} custom-call(f32[2048,1024]{1,0:T(8,128)} %bitcast.4), custom_call_target="tpu_custom_call" | custom-call | tf_op jit(solution)/shard_map/gram/pallas_call | solution.py:148
  34.2 15.4 %basis.1 = (f32[48,256]{1,0:T(8,128)}, f32[48,48]{1,0:T(8,128)}) custom-call(f32[256,256]{1,0:T(8,128)} %gram.1.gram_ref, f32[48,256]{1,0:T(8,128)} %bitcast.8), custom_call_target="tpu_custom_call" | custom-call | tf_op jit(solution)/shard_map/basis/pallas_call | solution.py:410
  49.5 102.5 %fit.1 = (f32[4,8,104,512]{3,2,1,0:T(8,128)}, f32[32,128]{1,0:T(8,128)}) custom-call(f32[2048,1024]{1,0:T(8,128)} %bitcast.5, f32[2048,512]{1,0:T(8,128)} %bitcast.6, f32[48,256]{1,0:T(8,128)} %get-tuple-element.9.basis_t, f32[48,48]{1,0:T(8,128)} %get-tuple-element.10.solver), custom_call_target="tpu_custom_call" | custom-call | tf_op jit(solution)/shard_map/fit/pallas_call | solution.py:307
  152.1 12.4 %correct.1 = f32[2048,512]{1,0:T(8,128)} custom-call(f32[2048,512]{1,0:T(8,128)} %bitcast.7, f32[4,8,104,512]{3,2,1,0:T(8,128)} %get-tuple-element.11.eigen, f32[32,128]{1,0:T(8,128)} %get-tuple-element.12.weights), custom_call_target="tpu_custom_call" | custom-call | tf_op jit(solution)/shard_map/correct/pallas_call | solution.py:360

commit v3 on v2

--- a/solution.py
+++ b/solution.py
@@ -53,6 +53,8 @@
 
 
 LANES = 128
+AHEAD = 4
+ROW_GROUP = 4
 
 
 def load_strips(source, target, sems):
@@ -84,13 +86,15 @@
         copies[c].wait()
         copies[c + 1].wait()
 
-        def one_row(r, carry):
-            here = strided_row(x, r, frames, rows, (c, c + 1))
+        def some_rows(turn, carry):
+            here = jnp.concatenate(
+                [strided_row(x, turn * ROW_GROUP + i, frames, rows, (c, c + 1))
+                 for i in range(ROW_GROUP)], axis=1)
             high, low = split(here - jnp.mean(here, axis=0, keepdims=True))
             acc[...] += dot_nt(high, high)
             cross[...] += dot_nt(high, low)
             return carry
-        lax.fori_loop(0, rows, one_row, 0)
+        lax.fori_loop(0, rows // ROW_GROUP, some_rows, 0)
     both = cross[...]
     acc[...] += both + both.T
     if not reduce_here:
@@ -218,12 +222,22 @@
     def cut_for(q):
         return e_rows.at[q // share, :, pl.ds(pl.multiple_of(lax.rem(q, share) * wide, wide), wide)]
 
+    def partner(e):
+        q = p
+        for bit in range(pix.bit_length() - 1):
+            if (e >> bit) % 2:
+                q = q + (1 << bit) * (1 - 2 * lax.rem(p // (1 << bit), 2))
+        return q
+
+    def send_columns(e):
+        q = partner(e)
+        second.append(send(cut_for(q), e_all.at[a, p], s2.at[e], r2.at[e], (a, q)))
+
     keep = pltpu.make_async_copy(cut_for(p), e_all.at[a, p], keep_sem)
     keep.start()
     second = []
-    for e in range(1, pix):
-        q = lax.rem(p + e, pix)
-        second.append(send(cut_for(q), e_all.at[a, p], s2.at[e], r2.at[e], (a, q)))
+    for e in range(1, AHEAD + 1):
+        send_columns(e)
     keep.wait()
 
     def add_fit(x_at, q):
@@ -246,6 +260,8 @@
     def pass_on(e, q):
         if e:
             second[e - 1].wait_recv()
+            if e + AHEAD < pix:
+                send_columns(e + AHEAD)
         piece = e_all.at[a, q]
         to_across.append(send(piece, piece, s3.at[0, e], r3.at[0, e], (across, p)))
         to_along.append(send(piece, piece, s3.at[1, e], r3.at[1, e], (along, p)))
@@ -273,7 +289,7 @@
         for lag, stage in enumerate((pass_on, forward, complete)):
             e = step - lag
             if 0 <= e < pix:
-                stage(e, lax.rem(p + pix - e, pix))
+                stage(e, partner(e))
     third = to_across + to_along + on_top + on_bottom
     sums = fit[...]
     part[...] = jnp.zeros_like(part)
@@ -350,7 +366,7 @@
                 at = pl.ds(q * rows + x_at * quarter + i, angles, stride=all_rows)
                 out[at, :] = proj[at, :] / jnp.maximum(estimate, floor_value)
         return carry
-    lax.fori_loop(0, pix, finish, 0)
+    lax.fori_loop(0, pix, finish, 0, unroll=4)
 
 
 def correct(projections, eigen, weights, rows, modes):

time: 165 us -> 149 us (0.903)
  Pallas kernels: 164 us -> 149 us
    pallas_call x1, Pallas kernels: 103 us -> 94.6 us  [fit_weights(): pl.pallas_call(functools.partial(fit_kernel, ang, pix, frames, rows, angl...]
    pallas_call x1, Pallas kernels: 34.2 us -> 28 us  [gram_of(): pl.pallas_call(functools.partial(gram_kernel, ang, pix, frames, rows, red...]
where the time goes in v3:
time: 149 us
  Pallas kernels  149 us (100%)
    pallas_call x1, Pallas kernels, fit_weights(): pl.pallas_call(functools.partial(fit_kernel, ang, pix, frames, rows, angl...  94.6 us
    pallas_call x1, Pallas kernels, gram_of(): pl.pallas_call(functools.partial(gram_kernel, ang, pix, frames, rows, red...  28 us
    pallas_call x1, Pallas kernels, basis_of(): pl.pallas_call(functools.partial(basis_kernel, npix), out_shape=(jax.Shap...  15.4 us
    pallas_call x1, Pallas kernels, correct(): pl.pallas_call(functools.partial(correct_kernel, ang, pix, rows, modes),...  10.8 us

profile of v3, /device:TPU:0, one launch (start us, length us, event | category | flops | bytes accessed | tf_op | source)
XLA Modules:
  0.0 148.8 jit_solution(16182952552786489326)
XLA Ops:
  0.0 28.0 %gram.1.gram_ref = f32[256,256]{1,0:T(8,128)} custom-call(f32[2048,1024]{1,0:T(8,128)} %bitcast.4), custom_call_target="tpu_custom_call" | custom-call | tf_op jit(solution)/shard_map/gram/pallas_call | solution.py:152
  28.0 15.4 %basis.1 = (f32[48,256]{1,0:T(8,128)}, f32[48,48]{1,0:T(8,128)}) custom-call(f32[256,256]{1,0:T(8,128)} %gram.1.gram_ref, f32[48,256]{1,0:T(8,128)} %bitcast.8), custom_call_target="tpu_custom_call" | custom-call | tf_op jit(solution)/shard_map/basis/pallas_call | solution.py:426
  43.4 94.6 %fit.1 = (f32[4,8,104,512]{3,2,1,0:T(8,128)}, f32[32,128]{1,0:T(8,128)}) custom-call(f32[2048,1024]{1,0:T(8,128)} %bitcast.5, f32[2048,512]{1,0:T(8,128)} %bitcast.6, f32[48,256]{1,0:T(8,128)} %get-tuple-element.9.basis_t, f32[48,48]{1,0:T(8,128)} %get-tuple-element.10.solver), custom_call_target="tpu_custom_call" | custom-call | tf_op jit(solution)/shard_map/fit/pallas_call | solution.py:323
  138.0 10.8 %correct.1 = f32[2048,512]{1,0:T(8,128)} custom-call(f32[2048,512]{1,0:T(8,128)} %bitcast.7, f32[4,8,104,512]{3,2,1,0:T(8,128)} %get-tuple-element.11.eigen, f32[32,128]{1,0:T(8,128)} %get-tuple-element.12.weights), custom_call_target="tpu_custom_call" | custom-call | tf_op jit(solution)/shard_map/correct/pallas_call | solution.py:376

commit v4 on v3

--- a/solution.py
+++ b/solution.py
@@ -175,8 +175,8 @@
 
 
 def fit_kernel(ang, pix, frames, rows, angles, all_rows, modes, npix,
-                   flats, projections, basis_t, solver, eigen_out, weights_out,
-                   x, proj, e_own, e_rows, e_all, fit, part, parts,
+                   flats, projections, gram_ref, start, eigen_out, weights_out,
+                   x, proj, solver, e_own, e_rows, e_all, fit, part, parts,
                    load_sem, proj_sem, store_sem, keep_sem, s1, r1, s2, r2, s3, r3, s4, r4):
     a, p = lax.axis_index("ang"), lax.axis_index("pix")
     greet(ang, pix, a, p)
@@ -188,7 +188,12 @@
     share = pix // ang
     e_own[...] = jnp.zeros_like(e_own)
     fit[...] = jnp.zeros_like(fit)
-    b_high, b_low = split(basis_t[...])
+    gram = gram_ref[...] / npix
+    basis_t = start[...]
+    for turn in range(SUBSPACE):
+        grown = dot_exact(basis_t, gram)
+        basis_t = dot_exact(inverse_factor(dot_nt(grown, grown, HIGHEST)), grown)
+    b_high, b_low = split(basis_t)
     b_both = jnp.concatenate([b_high, b_low], axis=0)
     for copy in copies:
         copy.wait()
@@ -214,6 +219,8 @@
         first.append(send(e_own.at[x_to], e_rows.at[a], s1.at[d], r1.at[d], (x_to, p)))
     eigen_rows(a)
     e_rows[a] = e_own[a]
+    normal = dot_nt(dot_exact(basis_t, gram), basis_t, HIGHEST)
+    solver[...] = inverse_factor(normal)
     for copy in proj_copies:
         copy.wait()
     for copy in first:
@@ -306,7 +313,7 @@
     fit_rhs = whole[:, :modes] / npix
     inner = dot_nt(fit_rhs, solver[...], HIGHEST)
     weights = jnp.dot(inner, solver[...], precision=HIGHEST, preferred_element_type=jnp.float32)
-    weights_out[...] = jnp.zeros_like(weights_out)
+    weights_out[...] = jnp.ones_like(weights_out)
     weights_out[:, :modes] = weights
     for copy in stores:
         copy.wait()
@@ -314,10 +321,10 @@
         copy.wait_send()
 
 
-def fit_weights(flats, projections, basis_t, solver, ang, pix, npix):
+def fit_weights(flats, projections, gram, start_basis, ang, pix, npix):
     frames, rows, cols = flats.shape
     angles, all_rows, wide = projections.shape
-    modes = basis_t.shape[0]
+    modes = start_basis.shape[1]
     unit = (rows // ang) * modes + 8
     vmem, dma = pltpu.VMEM, pltpu.SemaphoreType.DMA
     return pl.pallas_call(
@@ -331,6 +338,7 @@
         scratch_shapes=[
             vmem((cols // LANES, frames * rows, LANES), jnp.float32),
             vmem((wide // LANES, angles * all_rows, LANES), jnp.float32),
+            vmem((modes, modes), jnp.float32),
             vmem((ang, unit, cols), jnp.float32),
             vmem((ang, unit, cols), jnp.float32),
             vmem((ang, pix, unit, wide), jnp.float32),
@@ -346,47 +354,58 @@
         ),
         name="fit",
     )(flats.reshape(frames * rows, cols), projections.reshape(angles * all_rows, wide),
-      basis_t, solver)
-
-
-def correct_kernel(ang, pix, rows, modes, proj, eigen, weights, out):
+      gram, start_basis.T)
+
+
+def correct_kernel(rows, modes, proj, eigen, weights, out, spread_high, spread_low):
     angles = weights.shape[0]
-    all_rows = proj.shape[0] // angles
+    ang, _, unit, wide = eigen.shape
     quarter = rows // ang
-    w_high, w_low = split(weights[:, :modes])
-    w_all = jnp.concatenate([w_high, w_low, w_high], axis=1)
-
-    def finish(q, carry):
-        for x_at in range(ang):
-            for i in range(quarter):
-                mean = eigen[x_at, q, quarter * modes + i:quarter * modes + i + 1, :]
-                e_high, e_low = split(eigen[x_at, q, i * modes:(i + 1) * modes, :])
-                e_cat = jnp.concatenate([e_high, e_high, e_low], axis=0)
-                estimate = mean + jnp.dot(w_all, e_cat, preferred_element_type=jnp.float32)
-                at = pl.ds(q * rows + x_at * quarter + i, angles, stride=all_rows)
-                out[at, :] = proj[at, :] / jnp.maximum(estimate, floor_value)
-        return carry
-    lax.fori_loop(0, pix, finish, 0, unroll=4)
+    tall, depth = angles * rows, ang * unit
+
+    @pl.when(pl.program_id(0) == 0)
+    def _():
+        column = lax.broadcasted_iota(jnp.int32, (LANES, depth), 1)
+        within = lax.rem(column, unit)
+        is_mean = within >= quarter * modes
+        source = jnp.where(is_mean, modes, lax.rem(within, modes))
+        pick = (source == lax.broadcasted_iota(jnp.int32, (LANES, depth), 0)).astype(jnp.bfloat16)
+        column = lax.broadcasted_iota(jnp.int32, (tall, depth), 1)
+        within = lax.rem(column, unit)
+        place = jnp.where(within >= quarter * modes, within - quarter * modes, within // modes)
+        row = lax.rem(lax.broadcasted_iota(jnp.int32, (tall, depth), 0), rows)
+        own = (place < quarter) & (column // unit * quarter + place == row)
+        every = jnp.broadcast_to(weights[...][:, None, :], (angles, rows, LANES))
+        for part, spread in zip(split(every.reshape(tall, LANES)), (spread_high, spread_low)):
+            laid = jnp.dot(part, pick, preferred_element_type=jnp.float32)
+            spread[...] = jnp.where(own, laid, 0.0).astype(jnp.bfloat16)
+
+    e_high, e_low = split(eigen[...].reshape(depth, wide))
+    estimate = jnp.dot(spread_high[...], e_high, preferred_element_type=jnp.float32)
+    estimate += jnp.dot(spread_low[...], e_high, preferred_element_type=jnp.float32)
+    estimate += jnp.dot(spread_high[...], e_low, preferred_element_type=jnp.float32)
+    floored = jnp.maximum(estimate, floor_value)
+    out[...] = proj[...] / floored.reshape(angles, rows, wide)
 
 
 def correct(projections, eigen, weights, rows, modes):
-    angles, all_rows, wide = projections.shape
+    angles, _, wide = projections.shape
     ang, pix, unit, _ = eigen.shape
-    strip = pl.BlockSpec((angles * all_rows, LANES), lambda c: (0, c))
-    out = pl.pallas_call(
-        functools.partial(correct_kernel, ang, pix, rows, modes),
-        grid=(wide // LANES,),
-        out_shape=jax.ShapeDtypeStruct((angles * all_rows, wide), jnp.float32),
+    frame = pl.BlockSpec((angles, rows, wide), lambda q: (0, q, 0))
+    return pl.pallas_call(
+        functools.partial(correct_kernel, rows, modes),
+        grid=(pix,),
+        out_shape=jax.ShapeDtypeStruct(projections.shape, jnp.float32),
         in_specs=[
-            strip,
-            pl.BlockSpec((ang, pix, unit, LANES), lambda c: (0, 0, 0, c)),
-            pl.BlockSpec((angles, LANES), lambda c: (0, 0)),
+            frame,
+            pl.BlockSpec((ang, 1, unit, wide), lambda q: (0, q, 0, 0)),
+            pl.BlockSpec((angles, LANES), lambda q: (0, 0)),
         ],
-        out_specs=strip,
+        out_specs=frame,
+        scratch_shapes=[pltpu.VMEM((angles * rows, ang * unit), jnp.bfloat16)] * 2,
         compiler_params=pltpu.CompilerParams(vmem_limit_bytes=VMEM_LIMIT),
         name="correct",
-    )(projections.reshape(angles * all_rows, wide), eigen, weights)
-    return out.reshape(projections.shape)
+    )(projections, eigen, weights)
 
 
 def inverse_factor(matrix):
@@ -410,38 +429,13 @@
     return jnp.dot(a, b, precision=HIGHEST, preferred_element_type=jnp.float32)
 
 
-def basis_kernel(npix, gram_ref, start, basis_t, solver):
-    gram = gram_ref[...] / npix
-    basis = start[...]
-    for turn in range(SUBSPACE):
-        grown = dot_exact(basis, gram)
-        basis = dot_exact(inverse_factor(dot_nt(grown, grown, HIGHEST)), grown)
-    basis_t[...] = basis
-    normal = dot_nt(dot_exact(basis, gram), basis, HIGHEST)
-    solver[...] = inverse_factor(normal)
-
-
-def basis_of(gram, start_basis, npix):
-    modes = start_basis.shape[1]
-    return pl.pallas_call(
-        functools.partial(basis_kernel, npix),
-        out_shape=(
-            jax.ShapeDtypeStruct(start_basis.shape[::-1], jnp.float32),
-            jax.ShapeDtypeStruct((modes, modes), jnp.float32),
-        ),
-        compiler_params=pltpu.CompilerParams(vmem_limit_bytes=VMEM_LIMIT),
-        name="basis",
-    )(gram, start_basis.T)
-
-
 def shards(flats, projections, start_basis):
     rows_dev, cols_dev = flats.shape[1:]
     ang, pix = lax.axis_size("ang"), lax.axis_size("pix")
     npix = rows_dev * cols_dev * ang * pix
     gram = gram_of(flats, ang, pix)
-    basis_t, solver = basis_of(gram, start_basis, npix)
-    eigen, weights = fit_weights(flats, projections, basis_t, solver, ang, pix, npix)
-    return correct(projections, eigen, weights, rows_dev, basis_t.shape[0])
+    eigen, weights = fit_weights(flats, projections, gram, start_basis, ang, pix, npix)
+    return correct(projections, eigen, weights, rows_dev, start_basis.shape[1])
 
 
 def solution(mesh):

time: 149 us -> 141 us (0.946)
  Pallas kernels: 149 us -> 141 us
    pallas_call x2 -> x1, Pallas kernels: 26.1 us -> 10.3 us  [correct(): pl.pallas_call(functools.partial(correct_kernel, rows, modes), grid=(pix,...]
    pallas_call x1, Pallas kernels: 94.6 us -> 102 us  [fit_weights(): pl.pallas_call(functools.partial(fit_kernel, ang, pix, frames, rows, angl...]
where the time goes in v4:
time: 141 us
  Pallas kernels  141 us (100%)
    pallas_call x1, Pallas kernels, fit_weights(): pl.pallas_call(functools.partial(fit_kernel, ang, pix, frames, rows, angl...  102 us
    pallas_call x1, Pallas kernels, gram_of(): pl.pallas_call(functools.partial(gram_kernel, ang, pix, frames, rows, red...  28.1 us
    pallas_call x1, Pallas kernels, correct(): pl.pallas_call(functools.partial(correct_kernel, rows, modes), grid=(pix,...  10.3 us

profile of v4, /device:TPU:0, one launch (start us, length us, event | category | flops | bytes accessed | tf_op | source)
XLA Modules:
  0.0 140.7 jit_solution(13532919986665679620)
XLA Ops:
  0.0 28.1 %gram.1.gram_ref = f32[256,256]{1,0:T(8,128)} custom-call(f32[2048,1024]{1,0:T(8,128)} %bitcast.3), custom_call_target="tpu_custom_call" | custom-call | tf_op jit(solution)/shard_map/gram/pallas_call | solution.py:152
  28.1 102.4 %fit.1 = (f32[4,8,104,512]{3,2,1,0:T(8,128)}, f32[32,128]{1,0:T(8,128)}) custom-call(f32[2048,1024]{1,0:T(8,128)} %bitcast.4, f32[2048,512]{1,0:T(8,128)} %bitcast.5, f32[256,256]{1,0:T(8,128)} %gram.1.gram_ref, f32[48,256]{1,0:T(8,128)} %bitcast.6), custom_call_target="tpu_custom_call" | custom-call | tf_op jit(solution)/shard_map/fit/pallas_call | solution.py:330
  130.5 10.3 %correct.1 = f32[32,64,512]{2,1,0:T(8,128)} custom-call(f32[32,64,512]{2,1,0:T(8,128)} %proj.1, f32[4,8,104,512]{3,2,1,0:T(8,128)} %get-tuple-element.7.eigen, f32[32,128]{1,0:T(8,128)} %get-tuple-element.8.weights), custom_call_target="tpu_custom_call" | custom-call | tf_op jit(solution)/shard_map/correct/pallas_call | solution.py:395

commit v5 on v4

--- a/solution.py
+++ b/solution.py
@@ -365,16 +365,14 @@
 
     @pl.when(pl.program_id(0) == 0)
     def _():
-        column = lax.broadcasted_iota(jnp.int32, (LANES, depth), 1)
+        column = lax.broadcasted_iota(jnp.int32, (1, depth), 1)
         within = lax.rem(column, unit)
         is_mean = within >= quarter * modes
         source = jnp.where(is_mean, modes, lax.rem(within, modes))
         pick = (source == lax.broadcasted_iota(jnp.int32, (LANES, depth), 0)).astype(jnp.bfloat16)
-        column = lax.broadcasted_iota(jnp.int32, (tall, depth), 1)
-        within = lax.rem(column, unit)
         place = jnp.where(within >= quarter * modes, within - quarter * modes, within // modes)
-        row = lax.rem(lax.broadcasted_iota(jnp.int32, (tall, depth), 0), rows)
-        own = (place < quarter) & (column // unit * quarter + place == row)
+        row = lax.rem(lax.broadcasted_iota(jnp.int32, (tall, 1), 0), rows)
+        own = jnp.where(place < quarter, column // unit * quarter + place, -1) == row
         every = jnp.broadcast_to(weights[...][:, None, :], (angles, rows, LANES))
         for part, spread in zip(split(every.reshape(tall, LANES)), (spread_high, spread_low)):
             laid = jnp.dot(part, pick, preferred_element_type=jnp.float32)
@@ -418,9 +416,8 @@
     table = jnp.concatenate([matrix, gap, unit, gap], axis=1)
     below = lax.broadcasted_iota(jnp.int32, (order, 1), 0)
     for j in range(order - 1):
-        row = table[j:j + 1, :]
-        factor = table[:, j:j + 1] / table[j:j + 1, j:j + 1]
-        table = table - jnp.where(below > j, factor, 0.0) * row
+        row = table[j:j + 1, :] / table[j:j + 1, j:j + 1]
+        table = table - jnp.where(below > j, table[:, j:j + 1], 0.0) * row
     pivots = jnp.sum(table[:, :order] * unit, axis=1, keepdims=True)
     return table[:, side:side + order] / jnp.sqrt(pivots)
 

time: 141 us -> 141 us (level)
  no operation moved by 1% of the time
where the time goes in v5:
time: 141 us
  Pallas kernels  141 us (100%)
    pallas_call x1, Pallas kernels, fit_weights(): pl.pallas_call(functools.partial(fit_kernel, ang, pix, frames, rows, angl...  102 us
    pallas_call x1, Pallas kernels, gram_of(): pl.pallas_call(functools.partial(gram_kernel, ang, pix, frames, rows, red...  28.1 us
    pallas_call x1, Pallas kernels, correct(): pl.pallas_call(functools.partial(correct_kernel, rows, modes), grid=(pix,...  10.3 us

profile of v5, /device:TPU:0, one launch (start us, length us, event | category | flops | bytes accessed | tf_op | source)
XLA Modules:
  0.0 140.7 jit_solution(8667140279578302579)
XLA Ops:
  0.0 28.1 %gram.1.gram_ref = f32[256,256]{1,0:T(8,128)} custom-call(f32[2048,1024]{1,0:T(8,128)} %bitcast.3), custom_call_target="tpu_custom_call" | custom-call | tf_op jit(solution)/shard_map/gram/pallas_call | solution.py:152
  28.1 102.4 %fit.1 = (f32[4,8,104,512]{3,2,1,0:T(8,128)}, f32[32,128]{1,0:T(8,128)}) custom-call(f32[2048,1024]{1,0:T(8,128)} %bitcast.4, f32[2048,512]{1,0:T(8,128)} %bitcast.5, f32[256,256]{1,0:T(8,128)} %gram.1.gram_ref, f32[48,256]{1,0:T(8,128)} %bitcast.6), custom_call_target="tpu_custom_call" | custom-call | tf_op jit(solution)/shard_map/fit/pallas_call | solution.py:330
  130.5 10.3 %correct.1 = f32[32,64,512]{2,1,0:T(8,128)} custom-call(f32[32,64,512]{2,1,0:T(8,128)} %proj.1, f32[4,8,104,512]{3,2,1,0:T(8,128)} %get-tuple-element.7.eigen, f32[32,128]{1,0:T(8,128)} %get-tuple-element.8.weights), custom_call_target="tpu_custom_call" | custom-call | tf_op jit(solution)/shard_map/correct/pallas_call | solution.py:393
